TPU v7x, 512 devices: a whole 4x4x16 slice. The times are simulated.
512 devices in a mesh: ctx: 32 (over y, x, core), tp: 16 (over z).
Axes of the slice: x: 4, y: 4, z: 16, core: 2. Of those that a mesh axis runs over, the one named last changes fastest.
Arguments:
- queries: bfloat16 [8192, 4096], P('ctx', 'tp'), may hold values from -6 to 6
- keys: bfloat16 [8192, 2048], P('ctx', 'tp'), may hold values from -6 to 6
- values: bfloat16 [8192, 2048], P('ctx', 'tp'), may hold values from -6 to 6
- out_weight: bfloat16 [4096, 5120], P('tp'), may hold values from -0.09375 to 0.09375
- residual: bfloat16 [8192, 5120], P(('ctx', 'tp')), may hold values from -6 to 6
- norm_gain: float32 [5120], replicated, may hold values from 0.5 to 1.5
- lengths: int32 [32], replicated, may hold values from 1 to 4096, as said below
- owner_blocks: int32 [32, 2], replicated, may hold values from 0 to 63, as said below
Outputs:
- mixed: bfloat16 [8192, 5120], P(('ctx', 'tp'))
Inputs may be any that keep to these rules, and one draw needn't show every extreme that they name: 32 positive lengths that sum to 8192; one is exactly 4096. `owner_blocks`: every block number 0 to 63 appears exactly once; block b lies on index b // 2 of ctx, and the 2 blocks of one row lie on 2 different indices of ctx.
All inputs are finite; a program needn't handle non-finite values.
Results may differ from a plain program's by a relative error of at most 0.019.
Values may be sent and summed in bfloat16 or wider, within the bound.
A program may use at most 64 MiB of HBM per device.

v0:
```python
import math

import jax
import jax.numpy as jnp
from jax import lax
from jax.sharding import PartitionSpec as P

HD = 128
BLOCK = 128


FLOOR_SCORE = -1e30


def doc_index(positions, lengths):
    ends = jnp.cumsum(lengths)
    return jnp.sum((positions[:, None] >= ends[None, :]).astype(jnp.int32), axis=1)


def keep_state(run_state):
    return run_state


def make_attend(rows_q, q_pos, q_doc, lengths):
    scale = 1.0 / math.sqrt(HD)

    def attend(state_in, key_piece, value_piece, begin_at):
        how_many = key_piece.shape[0]
        sub_len = math.gcd(how_many, 1024)

        def sub_step(block_index, run_state):
            offset = block_index * sub_len
            key_block = lax.dynamic_slice_in_dim(key_piece, offset, sub_len)
            value_block = lax.dynamic_slice_in_dim(value_piece, offset, sub_len)
            k_pos = offset + jnp.arange(sub_len, dtype=jnp.int32)
            k_doc = doc_index(k_pos, lengths)
            visible = (
                (k_pos[None, :] <= q_pos[:, None])
                & (k_doc[None, :] == q_doc[:, None])
                & (k_pos[None, :] >= 0)
            )

            def update(current):
                run_max, run_sum, run_acc = current
                scores = (
                    jnp.einsum("qhd,kd->hqk", rows_q, key_block, preferred_element_type=jnp.float32)
                    * scale
                )
                scores = jnp.where(visible[None], scores, FLOOR_SCORE)
                new_max = jnp.maximum(run_max, jnp.max(scores, axis=2))
                weights = jnp.where(visible[None], jnp.exp(scores - new_max[:, :, None]), 0.0)
                rescale = jnp.exp(run_max - new_max)
                new_sum = run_sum * rescale + jnp.sum(weights, axis=2)
                new_acc = run_acc * rescale[:, :, None] + jnp.einsum(
                    "hqk,kd->hqd",
                    weights.astype(jnp.bfloat16),
                    value_block,
                    preferred_element_type=jnp.float32,
                )
                return (new_max, new_sum, new_acc)

            return lax.cond(jnp.any(visible), update, keep_state, run_state)

        return lax.fori_loop(0, how_many // sub_len, sub_step, state_in)

    return attend


def finish(state, tok_dev, q_width):
    run_max, run_sum, run_acc = state
    context = run_acc / run_sum[:, :, None]
    return jnp.transpose(context, (1, 0, 2)).reshape(tok_dev, q_width).astype(jnp.bfloat16)


def per_device(queries, keys, values, out_weight, residual, norm_gain, lengths, owner_blocks):
    ctx_size = lax.axis_size("ctx")
    my_rank = lax.axis_index("ctx")
    tok_dev = queries.shape[0]
    q_width = queries.shape[1]
    head_count = q_width // HD
    blocks_dev = tok_dev // BLOCK
    total_blocks = ctx_size * blocks_dev
    flat_owner = owner_blocks.reshape(-1)
    my_blocks = lax.dynamic_slice_in_dim(flat_owner, my_rank * blocks_dev, blocks_dev)
    local_ids = my_rank * blocks_dev + jnp.arange(blocks_dev, dtype=jnp.int32)
    sources = my_blocks // blocks_dev
    start_state = (
        jnp.full((head_count, tok_dev), FLOOR_SCORE, jnp.float32),
        jnp.zeros((head_count, tok_dev), jnp.float32),
        jnp.zeros((head_count, tok_dev, HD), jnp.float32),
    )
    placement = (flat_owner[:, None] == local_ids[None, :]).astype(jnp.bfloat16)
    outgoing = jnp.dot(
        placement, queries.reshape(blocks_dev, BLOCK * q_width), preferred_element_type=jnp.float32
    ).astype(jnp.bfloat16)
    incoming = lax.all_to_all(
        outgoing.reshape(total_blocks, BLOCK, q_width),
        "ctx",
        split_axis=0,
        concat_axis=0,
        tiled=True,
    )
    pick_rows = sources * blocks_dev + jnp.arange(blocks_dev, dtype=jnp.int32)
    owned_rows = jnp.take(incoming, pick_rows, axis=0)
    owned_rows = owned_rows.reshape(tok_dev, head_count, HD)
    q_pos = (my_blocks[:, None] * BLOCK + jnp.arange(BLOCK, dtype=jnp.int32)[None, :]).reshape(-1)
    q_doc = doc_index(q_pos, lengths)
    attend = make_attend(owned_rows, q_pos, q_doc, lengths)
    state = attend(
        start_state,
        lax.all_gather(keys, "ctx", axis=0, tiled=True),
        lax.all_gather(values, "ctx", axis=0, tiled=True),
        jnp.int32(0),
    )
    attended = finish(state, tok_dev, q_width)
    projected = lax.psum_scatter(
        jnp.dot(attended, out_weight, preferred_element_type=jnp.float32).astype(jnp.bfloat16),
        "tp",
        scatter_dimension=0,
        tiled=True,
    ).astype(jnp.float32)
    mean_sq = jnp.mean(projected * projected, axis=1, keepdims=True)
    normed = projected * lax.rsqrt(mean_sq + 1e-06) * norm_gain
    return (residual.astype(jnp.float32) + normed).astype(jnp.bfloat16)


def solution(mesh):
    in_specs = (
        P("ctx", "tp"),
        P("ctx", "tp"),
        P("ctx", "tp"),
        P("tp", None),
        P(("ctx", "tp"), None),
        P(),
        P(),
        P(),
    )
    out_specs = P(("ctx", "tp"), None)
    return jax.shard_map(
        per_device, mesh=mesh, in_specs=in_specs, out_specs=out_specs, check_vma=False
    )
```

profile of v0, /device:TPU:6, one launch (start us, length us, event | category | flops | bytes accessed | tf_op | source)
XLA Modules:
  0.0 288.6 jit_solution(18090017309957552272)
XLA Ops:
  10.4 3.1 %copy.20 = bf16[8,8,128,256]{3,2,1,0:T(8,128)(2,1)} copy(bf16[8,8,128,256]{3,1,2,0:T(8,128)(2,1)S(1)} %bitcast.42) | data formatting | bytes 8388608
  13.5 10.4 %all-to-all-start = ((bf16[64,128,256]{2,1,0:T(8,128)(2,1)}), bf16[64,128,256]{2,1,0:T(8,128)(2,1)}, u32[]{:S(2)}, u32[]{:S(2)}) async-start(bf16[64,128,256]{2,1,0:T(8,128)(2,1)} %bitcast.41), calls=%async_computation | async-start | bytes 8388608 | tf_op jit(solution)/shard_map/all_to_all | solution.py:96
  25.4 48.1 %all-to-all-done = bf16[64,128,256]{2,1,0:T(8,128)(2,1)} async-done(((bf16[64,128,256]{2,1,0:T(8,128)(2,1)}), bf16[64,128,256]{2,1,0:T(8,128)(2,1)}, u32[]{:S(2)}, u32[]{:S(2)}) %all-to-all-start) | async-done | bytes 4194336 | tf_op jit(solution)/shard_map/all_to_all | solution.py:96
  73.5 2.7 gather_fusion
  76.6 22.0 %all-gather.3.cloned.1.call-done = bf16[8192,128]{1,0:T(8,128)(2,1)} async-done(((bf16[256,128]{1,0:T(8,128)(2,1)}), bf16[8192,128]{1,0:T(8,128)(2,1)}) %all-gather.3.cloned.1.call-update) | async-done | bytes 2097168 | tf_op jit(solution)/shard_map/all_gather | solution.py:111
  98.6 61.6 %all-gather.5.cloned.1.call-done = bf16[8192,128]{1,0:T(8,128)(2,1)} async-done(((bf16[256,128]{1,0:T(8,128)(2,1)}), bf16[8192,128]{1,0:T(8,128)(2,1)}) %all-gather.5.cloned.1.call-update) | async-done | bytes 2097168 | tf_op jit(solution)/shard_map/all_gather | solution.py:112
  160.3 41.9 %while.20 = (s32[]{:T(128)}, f32[2,256]{1,0:T(2,128)S(1)}, f32[2,256]{1,0:T(2,128)S(1)}, f32[2,256,128]{2,1,0:T(8,128)S(1)}, s32[1,32]{1,0:T(1,128)S(1)}, /*inde...) while((s32[]{:T(128)}, f32[2,256]{1,0:T(2,128)S(1)}, ...), condition=%wide.region_9.10_spmd.clone, body=%wide.region_2.9_spmd.clone.sunk | while | flops 276794624 | bytes 8578489 | solution.py:64
  160.5 1.5 fusion.33
  162.6 3.9 %conditional.3 = ((f32[2,256]{1,0:T(2,128)S(1)}, f32[2,256]{1,0:T(2,128)S(1)}, f32[2,256,128]{2,1,0:T(8,128)S(1)})) conditional(s32[]{:T(128)} %convert_element_type.85, (f32[2,256]{1,0:T(2,128)S(1)}, f32[2,256]{1,0:T(2,128)S(1)}, f32[2,256,128]{2,1,0:T(8,128)S(1)}) %tuple.65, (pred[256,1024]{0,1:T(8,128)(4,1)S(1)}, s32[]{:T(128)}, ...), branch_computations={%region_5.5_spmd, %region_6.8_spmd} | conditional | flops 275383296 | bytes 8290378 | solution.py:62
  164.6 1.8 convolution_add_fusion
  166.7 1.5 fusion.33
  168.8 3.9 %conditional.3 = ((f32[2,256]{1,0:T(2,128)S(1)}, f32[2,256]{1,0:T(2,128)S(1)}, f32[2,256,128]{2,1,0:T(8,128)S(1)})) conditional(s32[]{:T(128)} %convert_element_type.85, (f32[2,256]{1,0:T(2,128)S(1)}, f32[2,256]{1,0:T(2,128)S(1)}, f32[2,256,128]{2,1,0:T(8,128)S(1)}) %tuple.65, (pred[256,1024]{0,1:T(8,128)(4,1)S(1)}, s32[]{:T(128)}, ...), branch_computations={%region_5.5_spmd, %region_6.8_spmd} | conditional | flops 275383296 | bytes 8290378 | solution.py:62
  170.8 1.8 convolution_add_fusion
  172.9 1.5 fusion.33
  175.0 3.9 %conditional.3 = ((f32[2,256]{1,0:T(2,128)S(1)}, f32[2,256]{1,0:T(2,128)S(1)}, f32[2,256,128]{2,1,0:T(8,128)S(1)})) conditional(s32[]{:T(128)} %convert_element_type.85, (f32[2,256]{1,0:T(2,128)S(1)}, f32[2,256]{1,0:T(2,128)S(1)}, f32[2,256,128]{2,1,0:T(8,128)S(1)}) %tuple.65, (pred[256,1024]{0,1:T(8,128)(4,1)S(1)}, s32[]{:T(128)}, ...), branch_computations={%region_5.5_spmd, %region_6.8_spmd} | conditional | flops 275383296 | bytes 8290378 | solution.py:62
  175.0 1.4 fusion.2
  177.0 1.8 convolution_add_fusion
  179.1 1.5 fusion.33
  181.2 3.9 %conditional.3 = ((f32[2,256]{1,0:T(2,128)S(1)}, f32[2,256]{1,0:T(2,128)S(1)}, f32[2,256,128]{2,1,0:T(8,128)S(1)})) conditional(s32[]{:T(128)} %convert_element_type.85, (f32[2,256]{1,0:T(2,128)S(1)}, f32[2,256]{1,0:T(2,128)S(1)}, f32[2,256,128]{2,1,0:T(8,128)S(1)}) %tuple.65, (pred[256,1024]{0,1:T(8,128)(4,1)S(1)}, s32[]{:T(128)}, ...), branch_computations={%region_5.5_spmd, %region_6.8_spmd} | conditional | flops 275383296 | bytes 8290378 | solution.py:62
  181.2 1.4 fusion.2
  183.2 1.8 convolution_add_fusion
  185.3 1.5 fusion.33
  187.4 3.9 %conditional.3 = ((f32[2,256]{1,0:T(2,128)S(1)}, f32[2,256]{1,0:T(2,128)S(1)}, f32[2,256,128]{2,1,0:T(8,128)S(1)})) conditional(s32[]{:T(128)} %convert_element_type.85, (f32[2,256]{1,0:T(2,128)S(1)}, f32[2,256]{1,0:T(2,128)S(1)}, f32[2,256,128]{2,1,0:T(8,128)S(1)}) %tuple.65, (pred[256,1024]{0,1:T(8,128)(4,1)S(1)}, s32[]{:T(128)}, ...), branch_computations={%region_5.5_spmd, %region_6.8_spmd} | conditional | flops 275383296 | bytes 8290378 | solution.py:62
  189.4 1.8 convolution_add_fusion
  191.5 1.5 fusion.33
  193.6 3.9 %conditional.3 = ((f32[2,256]{1,0:T(2,128)S(1)}, f32[2,256]{1,0:T(2,128)S(1)}, f32[2,256,128]{2,1,0:T(8,128)S(1)})) conditional(s32[]{:T(128)} %convert_element_type.85, (f32[2,256]{1,0:T(2,128)S(1)}, f32[2,256]{1,0:T(2,128)S(1)}, f32[2,256,128]{2,1,0:T(8,128)S(1)}) %tuple.65, (pred[256,1024]{0,1:T(8,128)(4,1)S(1)}, s32[]{:T(128)}, ...), branch_computations={%region_5.5_spmd, %region_6.8_spmd} | conditional | flops 275383296 | bytes 8290378 | solution.py:62
  195.6 1.8 convolution_add_fusion
  197.7 1.5 fusion.33
  200.0 1.5 fusion.33
  202.4 2.4 convolution_convert_fusion.1
  204.8 74.5 %reduce-scatter.2.cloned.1.call-done = bf16[16,5120]{1,0:T(8,128)(2,1)} async-done(((bf16[256,5120]{1,0:T(8,128)(2,1)}), bf16[16,5120]{1,0:T(8,128)(2,1)}) %reduce-scatter.2.cloned.1.call-update) | async-done | bytes 163856 | tf_op jit(solution)/shard_map/reduce_scatter | solution.py:116
  280.4 1.7 fusion.23
  (98 shorter events, 17.5 us)
Async XLA Ops:
  6.5 195.8 %copy-start = (bf16[256,5120]{1,0:T(8,128)(2,1)S(1)}, bf16[256,5120]{1,0:T(8,128)(2,1)}, u32[]{:S(2)}) copy-start(bf16[256,5120]{1,0:T(8,128)(2,1)} %param.15) | copy-start | bytes 7864324
  6.5 92.0 %all-gather.3.cloned.1.call-start = ((), (), s32[]{:S(2)}) async-start(), calls=%async_computation.2 | async-start | bytes 2162688 | tf_op jit(solution)/shard_map/all_gather | solution.py:111
  13.5 11.3 %copy-start.3 = (s32[32]{0:T(128)S(1)}, s32[32]{0:T(128)}, u32[]{:S(2)}) copy-start(s32[32]{0:T(128)} %param.18) | copy-start | bytes 388
  13.5 60.0 %all-to-all-start = ((bf16[64,128,256]{2,1,0:T(8,128)(2,1)}), bf16[64,128,256]{2,1,0:T(8,128)(2,1)}, u32[]{:S(2)}, u32[]{:S(2)}) async-start(bf16[64,128,256]{2,1,0:T(8,128)(2,1)} %bitcast.41), calls=%async_computation | async-start | bytes 8388608 | tf_op jit(solution)/shard_map/all_to_all | solution.py:96
  23.9 136.3 %all-gather.5.cloned.1.call-start = ((), (), s32[]{:S(2)}) async-start(), calls=%async_computation.3 | async-start | bytes 2162688 | tf_op jit(solution)/shard_map/all_gather | solution.py:112
  24.7 254.6 %reduce-scatter.2.cloned.1.call-start = ((), (), s32[]{:S(2)}) async-start(), calls=%async_computation.4 | async-start | bytes 2785280 | tf_op jit(solution)/shard_map/reduce_scatter | solution.py:116
  204.8 75.6 %copy-start.1 = (bf16[16,5120]{1,0:T(8,128)(2,1)S(1)}, bf16[16,5120]{1,0:T(8,128)(2,1)}, u32[]{:S(2)}) copy-start(bf16[16,5120]{1,0:T(8,128)(2,1)} %param.16) | copy-start | bytes 491524
  204.8 75.6 %copy-start.2 = (f32[5120]{0:T(1024)S(1)}, f32[5120]{0:T(1024)}, u32[]{:S(2)}) copy-start(f32[5120]{0:T(1024)} %param.17) | copy-start | bytes 61444
Sparse Core Ops, SparseCore 0:
  10.5 88.0 all-gather.2
  101.7 58.4 all-gather.4
  204.9 74.3 reduce-scatter.1
where the time goes:
time: 289 us
  waiting for transfers between devices  208 us (72%)
  matrix products  23.1 us (8%)
  other arithmetic  20.4 us (7%)
  between operations  13.3 us (5%)
  starting transfers between devices  10.5 us (4%)
  local copies, waits for them, and re-layouts  7.98 us (3%)
  loops' own time  5.82 us (2%)
    reduce_scatter x1, waiting for transfers between devices, per_device(): lax.psum_scatter(jnp.dot(attended, out_weight, preferred_element_type=jnp...  74.5 us
    all_gather x1, waiting for transfers between devices, per_device(): lax.all_gather(values, 'ctx', axis=0, tiled=True)  61.6 us
    all_to_all x1, waiting for transfers between devices, per_device(): lax.all_to_all(outgoing.reshape(total_blocks, BLOCK, q_width), 'ctx', spl...  48.1 us
    all_gather x1, waiting for transfers between devices, per_device(): lax.all_gather(keys, 'ctx', axis=0, tiled=True)  22 us
    reduce_or x8, other arithmetic, sub_step(): return lax.cond(jnp.any(visible), update, keep_state, run_state)  11.8 us
    dot_general x6, matrix products, update(): jnp.einsum('hqk,kd->hqd', weights.astype(jnp.bfloat16), value_block, pref...  11 us
    all_to_all x1, starting transfers between devices, per_device(): lax.all_to_all(outgoing.reshape(total_blocks, BLOCK, q_width), 'ctx', spl...  10.4 us
    dot_general x6, matrix products, update(): jnp.einsum('qhd,kd->hqk', rows_q, key_block, preferred_element_type=jnp.f...  8.47 us
  transfers between devices with their start and end apart: 4, of which 4 were waited for; matrix products, arithmetic and copies ran while one was open for 3% of the time, Pallas kernels for 0%

commit v1 on v0

v1 whole, which is shorter than its diff:
```python
import functools
import math

import jax
import jax.numpy as jnp
from jax import lax
from jax.experimental import pallas as pl
from jax.experimental.pallas import tpu as pltpu
from jax.sharding import PartitionSpec as P

MESH = pl.DeviceIdType.MESH

HD = 128
BLOCK = 128
TOK = 256
SIDE = 4
CHIPS = SIDE * SIDE
CT = 2 * TOK
PLANE = 2 * CHIPS
FLOOR = -1e30
SCALE = math.log2(math.e) / math.sqrt(HD)
BF = jnp.bfloat16
F32 = jnp.float32


def iota(shape, dim):
    return lax.broadcasted_iota(jnp.int32, shape, dim)


def kernel(
    nt,
    docs,
    q_hbm,
    k_hbm,
    v_hbm,
    w_hbm,
    res_hbm,
    gain_hbm,
    len_ref,
    own_ref,
    out_ref,
    qbuf,
    vtmp,
    kv,
    qt,
    acc,
    stat,
    send1,
    recv1,
    perm,
    send2,
    abuf,
    wbuf,
    part1,
    part2,
    sib_out,
    sib_in,
    osend,
    obuf,
    resv,
    gainv,
    loc_sem,
    q_sem,
    kv_send,
    kv_recv,
    sib_send,
    sib_recv,
    w_send,
    w_recv,
    a1_send,
    a1_recv,
    z_send,
    z_recv,
    ag_send,
    ag_recv,
    x_sem,
    fin_send,
    fin_recv,
):
    ni = nt // 2
    ext = 8 // ni
    rb = ext * 32
    orows = 16 * ext
    me = lax.axis_index("ctx")
    t = lax.axis_index("tp")
    c = me // 2
    h = me % 2
    sib = (me + 1 - 2 * h, t)
    x = c % SIDE
    y = c // SIDE
    u = x + h * (y - x)
    v = y + h * (x - y)

    def chip(uu, vv):
        return (uu % SIDE) * (1 + 3 * h) + (vv % SIDE) * (4 - 3 * h)

    def remote(src, dst, ssem, rsem, dev):
        return pltpu.make_async_remote_copy(
            src_ref=src, dst_ref=dst, send_sem=ssem, recv_sem=rsem, device_id=dev, device_id_type=MESH
        )

    head = pl.multiple_of(h * HD, HD)
    other_head = pl.multiple_of((1 - h) * HD, HD)
    my_w = pl.ds(pl.multiple_of(t * HD, HD), HD)
    col1 = pl.ds(pl.multiple_of(c * 256, 256), 256)
    col2 = pl.ds(pl.multiple_of(4096 + (c // 2) * 128, 128), 128)
    loads = [
        (k_hbm, kv.at[h, c, 0]),
        (v_hbm, vtmp),
        (q_hbm.at[:, pl.ds(head, HD)], qbuf.at[h]),
        (w_hbm.at[pl.ds(head, HD), col1], wbuf.at[my_w, pl.ds(0, 256)]),
        (w_hbm.at[pl.ds(head, HD), col2], wbuf.at[my_w, pl.ds(256, 128)]),
        (res_hbm, resv),
        (gain_hbm, gainv),
    ]
    loads = [pltpu.make_async_copy(s, d, loc_sem.at[n]) for n, (s, d) in enumerate(loads)]
    for copy in loads:
        copy.start()
    barrier = pltpu.get_barrier_semaphore()

    @pl.loop(1, PLANE)
    def _(d):
        pl.semaphore_signal(barrier, inc=1, device_id=((me + d) % PLANE, t), device_id_type=MESH)

    @pl.loop(1, nt)
    def _(d):
        pl.semaphore_signal(barrier, inc=1, device_id=(me, (t + d) % nt), device_id_type=MESH)

    row = iota((CT, 1), 0)
    target = (row % 16) * 32 + (row // BLOCK) * 8 + (row % BLOCK) // 16
    spread = jnp.where(iota((CT, CT), 1) == target, 1.0, 0.0).astype(BF)
    perm[...] = spread
    lane = iota((1, CT), 1)
    pos = c * CT + ((lane // 8) % 4) * BLOCK + (lane % 8) * 16 + lane // 32
    first = jnp.zeros((1, CT), jnp.int32)
    end = jnp.int32(0)
    for n in range(docs):
        end = end + len_ref[n]
        first = jnp.where(end <= pos, end, first)

    loads[0].wait()
    loads[1].wait()
    vt = vtmp[...].astype(F32)
    for n in range(TOK // HD):
        kv[h, c, 1, n * HD : (n + 1) * HD, :] = vt[n * HD : (n + 1) * HD, :].T.astype(BF)
    loads[2].wait()
    loads[3].wait()
    loads[4].wait()

    pl.semaphore_wait(barrier, PLANE - 1 + nt - 1)

    right = (me, (t + 1) % nt)
    left = (me, (t + nt - 1) % nt)
    rsteps = nt // 2
    lsteps = nt - 1 - rsteps

    def w_copy(way, step):
        slot = (t - step + nt) % nt if way == 0 else (t + step) % nt
        ref = wbuf.at[pl.ds(pl.multiple_of(slot * HD, HD), HD)]
        return remote(ref, ref, w_send.at[way, step], w_recv.at[way, step], right if way == 0 else left)

    def w_step(step):
        for way, count in ((0, rsteps), (1, lsteps)):
            if step >= 1 and step - 1 < count:
                w_copy(way, step - 1).wait_recv()
            if step < count:
                w_copy(way, step).start()

    def w_finish():
        for way, count in ((0, rsteps), (1, lsteps)):
            for step in range(count):
                w_copy(way, step).wait_send()

    def gather(buf, ssem, rsem, on_ready, pause):
        def full(src, to, n):
            return remote(buf.at[src], buf.at[src], ssem.at[n], rsem.at[src, 0], (to * 2 + h, t))

        def half(src, part, to, n):
            ref = buf.at[src, part]
            return remote(ref, ref, ssem.at[n], rsem.at[src, part], (to * 2 + h, t))

        sends = []

        def go(copy):
            copy.start()
            sends.append(copy)

        def onward(uu, n):
            src = chip(uu, v)
            go(full(src, chip(u, v + 1), n))
            go(full(src, chip(u, v + 3), n + 1))
            on_ready(src)

        go(full(c, chip(u + 1, v), 0))
        go(full(c, chip(u + 3, v), 1))
        onward(u, 2)
        pause(0)
        low = chip(u + 3, v)
        full(low, c, 4).wait_recv()
        go(half(low, 0, chip(u + 1, v), 4))
        high = chip(u + 1, v)
        full(high, c, 5).wait_recv()
        go(half(high, 1, chip(u + 3, v), 5))
        onward(u + 3, 6)
        onward(u + 1, 8)
        pause(1)
        far = chip(u + 2, v)
        half(far, 0, c, 10).wait_recv()
        half(far, 1, c, 10).wait_recv()
        onward(u + 2, 10)
        pause(2)
        n = 12
        for du in (0, 3, 1, 2):
            low = chip(u + du, v + 3)
            full(low, c, n).wait_recv()
            go(half(low, 0, chip(u, v + 1), n))
            on_ready(low)
            high = chip(u + du, v + 1)
            full(high, c, n + 1).wait_recv()
            go(half(high, 1, chip(u, v + 3), n + 1))
            on_ready(high)
            n += 2
            if du == 3:
                pause(3)
        pause(4)
        for du in (0, 3, 1, 2):
            far = chip(u + du, v + 2)
            half(far, 0, c, 0).wait_recv()
            half(far, 1, c, 0).wait_recv()
            on_ready(far)
        for copy in sends:
            copy.wait_send()

    def attend(src, start):
        keys = jnp.concatenate([kv[0, src, 0], kv[1, src, 0]], axis=0)
        pieces = []
        for core in range(2):
            block = kv[core, src, 1]
            pieces += [block[n * HD : (n + 1) * HD] for n in range(TOK // HD)]
        values = jnp.concatenate(pieces, axis=1)
        wide = 256
        for n in range(CT // wide):
            cols = slice(n * wide, (n + 1) * wide)
            score = jnp.dot(keys, qt[:, cols], preferred_element_type=F32) * SCALE
            kpos = src * CT + iota((CT, wide), 0)
            visible = kpos >= first[:, cols]
            if start:
                visible = visible & (kpos <= pos[:, cols])
            score = jnp.where(visible, score, FLOOR)
            top = jnp.max(score, axis=0, keepdims=True)
            if not start:
                old = stat[0:1, cols]
                top = jnp.maximum(top, old)
                decay = jnp.exp2(old - top)
            weight = jnp.exp2(score - top)
            total = jnp.sum(weight, axis=0, keepdims=True)
            context = jnp.dot(values, weight.astype(BF), preferred_element_type=F32)
            if not start:
                total = total + stat[1:2, cols] * decay
                context = context + acc[:, cols] * decay
            stat[0:1, cols] = top
            stat[1:2, cols] = total
            acc[:, cols] = context

    def swap_copy(src):
        ref = kv.at[h, src]
        return remote(ref, ref, sib_send.at[src], sib_recv.at[src], sib)

    def swap_wait(src):
        ref = kv.at[1 - h, src]
        remote(ref, ref, sib_send.at[src], sib_recv.at[src], sib).wait_recv()

    q_send = remote(q_hbm.at[:, pl.ds(other_head, HD)], qbuf.at[h], q_sem.at[0], q_sem.at[1], sib)
    q_send.start()

    def kv_ready(src):
        swap_copy(src).start()

    def kv_pause(n):
        if n == 0:
            w_step(0)
            q_send.wait_recv()
            for core in range(2):
                rows = qbuf[core].astype(F32).T.astype(BF)
                some = jnp.dot(rows, perm[core * TOK : (core + 1) * TOK, :], preferred_element_type=F32)
                if core == 0:
                    total = some
                else:
                    total = total + some
            qt[...] = total.astype(BF)
            swap_wait(c)
            attend(c, True)
        elif n < 5:
            w_step(n)

    gather(kv.at[h], kv_send, kv_recv, kv_ready, kv_pause)

    @pl.loop(1, CHIPS)
    def _(d):
        swap_wait((c + d) % CHIPS)

    @pl.loop(1, jnp.minimum(c, 8) + 1)
    def _(k):
        attend(c - k, False)

    w_step(5)
    result = (acc[...] / stat[1:2, :]).T.astype(BF)
    send1[...] = result

    def a1_copy(d):
        to = (c + d) % CHIPS
        return remote(
            send1.at[pl.ds(pl.multiple_of(to * 32, 32), 32)],
            recv1.at[pl.ds(pl.multiple_of(c * 32, 32), 32)],
            a1_send.at[d],
            a1_recv.at[d],
            (to * 2 + h, t),
        )

    @pl.loop(1, CHIPS)
    def _(d):
        a1_copy(d).start()

    mine = pl.ds(pl.multiple_of(c * 32, 32), 32)
    recv1[mine, :] = send1[mine, :]

    for k in range(2):
        owned = own_ref[:, k : k + 1] * 8
        for i in range(8):
            rows = slice((k * 8 + i) * 32, (k * 8 + i + 1) * 32)
            perm[rows, :] = jnp.where(iota((32, CT), 1) == owned + i, 1.0, 0.0).astype(BF)

    @pl.loop(1, CHIPS)
    def _(d):
        a1_copy(d).wait()

    send2[...] = jnp.dot(perm[...], recv1[...], preferred_element_type=F32).astype(BF)

    def z_dst():
        return abuf.at[c, t // ni, pl.ds(pl.multiple_of((t % ni) * rb, 32), rb)]

    def z_copy(d):
        to = (t + d) % nt
        return remote(
            send2.at[pl.ds(pl.multiple_of(to * rb, 32), rb)], z_dst(), z_send.at[d], z_recv.at[d], (me, to)
        )

    @pl.loop(1, nt)
    def _(d):
        z_copy(d).start()

    abuf[c, t // ni, pl.ds(pl.multiple_of((t % ni) * rb, 32), rb), :] = send2[
        pl.ds(pl.multiple_of(t * rb, 32), rb), :
    ]
    w_step(6)

    @pl.loop(1, nt)
    def _(d):
        z_copy(d).wait()

    def ag_pause(n):
        if n == 2:
            w_step(7)
        if n == 4:
            w_step(8)

    gather(abuf, ag_send, ag_recv, lambda src: None, ag_pause)
    w_finish()

    half_of = c % 2

    @pl.loop(0, SIDE)
    def _(g):
        lhs1 = []
        lhs2 = []
        for s in range(nt):
            base = (s % ni) * rb
            lhs1.append(abuf[pl.ds(g * 4, 4), s // ni, base : base + rb, :].reshape(4 * rb, HD))
            for e in range(ext):
                at = pl.ds(pl.multiple_of(base + e * 32 + half_of * 16, 16), 16)
                lhs2.append(abuf[pl.ds(g * 4, 4), s // ni, at, :])
        lhs1 = jnp.concatenate(lhs1, axis=1)
        cat = []
        for s in range(nt):
            cat.append(jnp.concatenate(lhs2[s * ext : (s + 1) * ext], axis=1).reshape(4 * ext * 16, HD))
        lhs2 = jnp.concatenate(cat, axis=1)
        product = jnp.dot(lhs1, wbuf[:, 0:256], preferred_element_type=F32)
        for core in range(2):
            part1[core, pl.ds(pl.multiple_of(g * 4 * rb, 128), 4 * rb), :] = product[:, core * HD : (core + 1) * HD]
        part2[pl.ds(pl.multiple_of(g * 2 * rb, 64), 2 * rb), :] = jnp.dot(
            lhs2, wbuf[:, 256:384], preferred_element_type=F32
        )

    def tile(n, core):
        out = []
        for e in range(ext):
            out.append(part1[core, pl.ds(e * 32 + n, 16, stride=rb), :])
        return out

    def tile2(n, core):
        out = []
        for e in range(ext):
            out.append(part2[pl.ds(e * 16 + core * 8 + n, 16, stride=rb // 2), :])
        return out

    def exchange(put, core):
        for n in range(32):
            for e, val in enumerate(tile(n, core)):
                put(n, e, val)
        for n in range(8):
            for e, val in enumerate(tile2(n, core)):
                put(32 + n, e, val)

    def put_sib(n, e, val):
        sib_out[n, e * 16 : (e + 1) * 16, :] = val.astype(BF)

    exchange(put_sib, 1 - h)
    x_copy = remote(sib_out, sib_in, x_sem.at[0], x_sem.at[1], sib)
    x_copy.start()
    x_copy.wait()

    def put_fin(n, e, val):
        rows = slice(e * 16, (e + 1) * 16)
        osend[n, rows, :] = (val + sib_in[n, rows, :].astype(F32)).astype(BF)

    exchange(put_fin, h)

    def fin_copy(d):
        to = (me + d) % PLANE
        return remote(osend.at[to], obuf.at[me], fin_send.at[d], fin_recv.at[d], (to, t))

    @pl.loop(1, PLANE)
    def _(d):
        fin_copy(d).start()

    base = half_of * 16 + h * 8
    shared = 32 + c // 2

    def fin2_copy(n):
        return remote(
            osend.at[32 + n], obuf.at[shared], fin_send.at[PLANE + n], fin_recv.at[PLANE + c // 2], (base + n, t)
        )

    @pl.loop(0, 8)
    def _(n):
        @pl.when(base + n != me)
        def _():
            fin2_copy(n).start()

    obuf[me] = osend[me]

    @pl.when((me >= base) & (me < base + 8))
    def _():
        obuf[shared] = osend[32 + jnp.clip(me - base, 0, 7)]

    loads[5].wait()
    loads[6].wait()

    @pl.loop(1, PLANE)
    def _(d):
        fin_copy(d).wait()

    @pl.loop(0, 8)
    def _(n):
        @pl.when(base + n != me)
        def _():
            fin2_copy(n).wait_send()

        @pl.when((2 * n + me // 16) * 2 + (me % 16) // 8 != me)
        def _():
            remote(osend.at[0], obuf.at[32 + n], fin_send.at[0], fin_recv.at[PLANE + n], sib).wait_recv()

    q_send.wait_send()

    @pl.loop(0, CHIPS)
    def _(n):
        swap_copy(n).wait_send()

    square = jnp.zeros((orows, HD), F32)
    for n in range(40):
        val = obuf[n].astype(F32)
        square = square + val * val
    mean = jnp.sum(square, axis=1, keepdims=True) / (40 * HD)
    factor = lax.rsqrt(mean + 1e-6)
    for n in range(40):
        cols = slice(n * HD, (n + 1) * HD)
        val = obuf[n].astype(F32) * factor * gainv[n : n + 1, :]
        out_ref[:, cols] = (resv[:, cols].astype(F32) + val).astype(BF)


def per_device(queries, keys, values, out_weight, residual, norm_gain, lengths, owner_blocks):
    nt = lax.axis_size("tp")
    docs = lengths.shape[0]
    width = out_weight.shape[1]
    ext = 16 // nt
    orows = 16 * ext
    any_spec = pl.BlockSpec(memory_space=pl.ANY)
    vmem = pltpu.VMEM
    dma = pltpu.SemaphoreType.DMA
    scratch = dict(
        qbuf=vmem((2, TOK, HD), BF),
        vtmp=vmem((TOK, HD), BF),
        kv=vmem((2, CHIPS, 2, TOK, HD), BF),
        qt=vmem((HD, CT), BF),
        acc=vmem((HD, CT), F32),
        stat=vmem((8, CT), F32),
        send1=vmem((CT, HD), BF),
        recv1=vmem((CT, HD), BF),
        perm=vmem((CT, CT), BF),
        send2=vmem((CT, HD), BF),
        abuf=vmem((CHIPS, 2, TOK, HD), BF),
        wbuf=vmem((nt * HD, 3 * HD), BF),
        part1=vmem((2, CT * ext, HD), F32),
        part2=vmem((CT * ext // 2, HD), F32),
        sib_out=vmem((40, orows, HD), BF),
        sib_in=vmem((40, orows, HD), BF),
        osend=vmem((40, orows, HD), BF),
        obuf=vmem((40, orows, HD), BF),
        resv=vmem((orows, width), BF),
        gainv=vmem((width // HD, HD), F32),
        loc_sem=dma((7,)),
        q_sem=dma((2,)),
        kv_send=dma((20,)),
        kv_recv=dma((CHIPS, 2)),
        sib_send=dma((CHIPS,)),
        sib_recv=dma((CHIPS,)),
        w_send=dma((2, 8)),
        w_recv=dma((2, 8)),
        a1_send=dma((CHIPS,)),
        a1_recv=dma((CHIPS,)),
        z_send=dma((16,)),
        z_recv=dma((16,)),
        ag_send=dma((20,)),
        ag_recv=dma((CHIPS, 2)),
        x_sem=dma((2,)),
        fin_send=dma((PLANE + 8,)),
        fin_recv=dma((PLANE + 8,)),
    )
    return pl.pallas_call(
        functools.partial(kernel, nt, docs),
        out_shape=jax.ShapeDtypeStruct((orows, width), BF),
        in_specs=[any_spec] * 6
        + [pl.BlockSpec(memory_space=pltpu.SMEM), pl.BlockSpec(memory_space=pltpu.VMEM)],
        out_specs=pl.BlockSpec(memory_space=pltpu.VMEM),
        scratch_shapes=list(scratch.values()),
        compiler_params=pltpu.CompilerParams(
            collective_id=0, has_side_effects=True, vmem_limit_bytes=48 * 1024 * 1024
        ),
        name="attend_project",
    )(
        queries,
        keys,
        values,
        out_weight,
        residual,
        norm_gain.reshape(width // HD, HD),
        lengths,
        owner_blocks,
    )


def solution(mesh):
    in_specs = (
        P("ctx", "tp"),
        P("ctx", "tp"),
        P("ctx", "tp"),
        P("tp", None),
        P(("ctx", "tp"), None),
        P(),
        P(),
        P(),
    )
    out_specs = P(("ctx", "tp"), None)
    return jax.shard_map(
        per_device, mesh=mesh, in_specs=in_specs, out_specs=out_specs, check_vma=False
    )
```

time: 289 us -> 99 us (0.34)
  the two profiles are of different devices: /device:TPU:6 before, /device:TPU:1 now
where the time goes in v1:
time: 99 us; the launch traced here: 98.6 us
  Pallas kernels  90.6 us (92%)
  local copies, waits for them, and re-layouts  8.05 us (8%)
    pallas_call x1, Pallas kernels, per_device(): pl.pallas_call(functools.partial(kernel, nt, docs), out_shape=jax.ShapeDt...  90.6 us
    unnamed x16, local copies, waits for them, and re-layouts  8.05 us

profile of v1, /device:TPU:1, one launch (start us, length us, event | category | flops | bytes accessed | tf_op | source)
XLA Modules:
  0.0 98.6 jit_solution(2863925350891404252)
XLA Ops:
  0.0 0.8 copy.9.own_ref
  0.8 0.0 copy-start
  0.8 1.7 %copy-done = bf16[256,5120]{1,0:T(8,128)(2,1)S(1)} copy-done((bf16[256,5120]{1,0:T(8,128)(2,1)S(1)}, bf16[256,5120]{1,0:T(8,128)(2,1)}, u32[]{:S(2)}) %copy-start) | copy-done | bytes 2621464
  2.5 0.0 copy-start.1
  2.5 0.9 copy-done.1
  3.4 0.0 copy-start.2
  3.4 0.9 copy-done.2
  4.3 0.0 copy-start.3
  4.3 0.8 copy-done.3
  5.2 0.0 copy-start.4
  5.2 0.8 copy-done.4
  6.0 0.0 copy-start.5
  6.0 0.7 copy-done.5
  6.7 0.0 copy-start.6
  6.7 0.7 copy-done.6
  7.4 90.6 %attend_project.1 = bf16[16,5120]{1,0:T(8,128)(2,1)S(1)} custom-call(bf16[256,256]{1,0:T(8,128)(2,1)S(1)} %copy-done.2, bf16[256,128]{1,0:T(8,128)(2,1)S(1)} %copy-done.3, bf16[256,128]{1,0:T(8,128)(2,1)S(1)} %copy-done.4, bf16[256,5120]{1,0:T(8,128)(2,1)S(1)} %copy-done, bf16[16,5120]{1,0:T(8,128)(2,1)S(1)} %copy-done.1, f32[40,128]{1,0:T(8,128)S(1)} %bitcast.1, ...), custom_call_target="tpu_custom_call" | custom-call | tf_op jit(solution)/shard_map/attend_project/pallas_call | solution.py:539
  97.9 0.7 copy.11
Async XLA Ops:
  0.8 1.7 %copy-start = (bf16[256,5120]{1,0:T(8,128)(2,1)S(1)}, bf16[256,5120]{1,0:T(8,128)(2,1)}, u32[]{:S(2)}) copy-start(bf16[256,5120]{1,0:T(8,128)(2,1)} %w_hbm.1) | copy-start | bytes 7864324
  2.5 0.9 copy-start.1
  3.4 0.9 copy-start.2
  4.3 0.8 copy-start.3
  5.2 0.8 copy-start.4
  6.0 0.7 copy-start.5
  6.7 0.7 copy-start.6

commit v2 on v1

v2 whole, which is shorter than its diff:
```python
import functools
import math

import jax
import jax.numpy as jnp
from jax import lax
from jax.experimental import pallas as pl
from jax.experimental.pallas import tpu as pltpu
from jax.sharding import PartitionSpec as P

MESH = pl.DeviceIdType.MESH

HD = 128
BLOCK = 128
TOK = 256
SIDE = 4
CHIPS = SIDE * SIDE
CT = 2 * TOK
PLANE = 2 * CHIPS
FLOOR = -1e30
SCALE = math.log2(math.e) / math.sqrt(HD)
BF = jnp.bfloat16
F32 = jnp.float32


def iota(shape, dim):
    return lax.broadcasted_iota(jnp.int32, shape, dim)


def kernel(
    nt,
    docs,
    q_hbm,
    k_hbm,
    v_hbm,
    w_hbm,
    res_hbm,
    gain_hbm,
    len_ref,
    own_ref,
    out_ref,
    qbuf,
    vtmp,
    kv,
    qt,
    acc,
    stat,
    send1,
    recv1,
    perm,
    perm2,
    send2,
    abuf,
    wbuf,
    part,
    xout,
    xin,
    osend,
    obuf,
    resv,
    gainv,
    hail_sem,
    loc_sem,
    q_sem,
    kv_send,
    fwd_send,
    kv_recv,
    sib_send,
    sib_recv,
    w_send,
    w_recv,
    a1_send,
    a1_recv,
    z_send,
    z_recv,
    ag_send,
    ag_recv,
    x_send,
    x_recv,
    fin_send,
    fin_recv,
):
    orows = out_ref.shape[0]
    me = lax.axis_index("ctx")
    t = lax.axis_index("tp")
    c = me // 2
    h = me % 2
    sib = (me + 1 - 2 * h, t)
    x = c % SIDE
    y = c // SIDE
    u = x + h * (y - x)
    v = y + h * (x - y)

    def chip(uu, vv):
        return (uu % SIDE) * (1 + 3 * h) + (vv % SIDE) * (4 - 3 * h)

    def remote(src, dst, ssem, rsem, dev):
        return pltpu.make_async_remote_copy(
            src_ref=src, dst_ref=dst, send_sem=ssem, recv_sem=rsem, device_id=dev, device_id_type=MESH
        )

    head = pl.multiple_of(h * HD, HD)
    other_head = pl.multiple_of((1 - h) * HD, HD)
    my_w = pl.ds(pl.multiple_of(t * HD, HD), HD)
    col1 = pl.ds(pl.multiple_of(c * 256, 256), 256)
    col2 = pl.ds(pl.multiple_of(4096 + (c // 2) * 128, 128), 128)
    loads = [
        (k_hbm, kv.at[h, c, 0]),
        (v_hbm, vtmp),
        (q_hbm.at[:, pl.ds(head, HD)], qbuf.at[h]),
        (w_hbm.at[pl.ds(head, HD), col1], wbuf.at[my_w, pl.ds(0, 256)]),
        (w_hbm.at[pl.ds(head, HD), col2], wbuf.at[my_w, pl.ds(256, 128)]),
        (res_hbm, resv),
        (gain_hbm, gainv),
    ]
    loads = [pltpu.make_async_copy(s, d, loc_sem.at[n]) for n, (s, d) in enumerate(loads)]
    for copy in loads:
        copy.start()
    barrier = pltpu.get_barrier_semaphore()

    @pl.loop(1, CHIPS)
    def _(d):
        pl.semaphore_signal(barrier, inc=1, device_id=((me + 2 * d) % PLANE, t), device_id_type=MESH)

    right = (me, (t + 1) % nt)
    left = (me, (t + nt - 1) % nt)
    for dev in (right, left, sib):
        pl.semaphore_signal(barrier, inc=1, device_id=dev, device_id_type=MESH)

    row = iota((CT, 1), 0)
    target = (row % 16) * 32 + (row // BLOCK) * 8 + (row % BLOCK) // 16
    spread = jnp.where(iota((CT, CT), 1) == target, 1.0, 0.0).astype(BF)
    perm[...] = spread
    lane = iota((1, CT), 1)
    pos = c * CT + ((lane // 8) % 4) * BLOCK + (lane % 8) * 16 + lane // 32
    first = jnp.zeros((1, CT), jnp.int32)
    end = jnp.int32(0)
    for n in range(docs):
        end = end + len_ref[n]
        first = jnp.where(end <= pos, end, first)

    for k in range(2):
        owned = jnp.zeros((PLANE, 1), jnp.int32)
        for o in range(PLANE):
            owned = jnp.where(iota((PLANE, 1), 0) == o, own_ref[k, o] * 8, owned)
        for i in range(8):
            rows = slice((k * 8 + i) * PLANE, (k * 8 + i + 1) * PLANE)
            perm2[rows, :] = jnp.where(iota((PLANE, CT), 1) == owned + i, 1.0, 0.0).astype(BF)

    loads[0].wait()
    loads[1].wait()
    vt = vtmp[...].astype(F32)
    for n in range(TOK // HD):
        kv[h, c, 1, n * HD : (n + 1) * HD, :] = vt[n * HD : (n + 1) * HD, :].T.astype(BF)
    loads[2].wait()
    loads[3].wait()
    loads[4].wait()

    pl.semaphore_wait(barrier, CHIPS + 2)

    def hail(n):
        for dev in ((me, (t + 2**n) % nt), (me, (t + nt - 2**n) % nt)):
            pl.semaphore_signal(hail_sem.at[n], inc=1, device_id=dev, device_id_type=MESH)

    def heard(n):
        pl.semaphore_wait(hail_sem.at[n], 2)

    hail(0)

    rsteps = nt // 2
    lsteps = nt - 1 - rsteps

    def w_copy(way, step):
        slot = (t - step + nt) % nt if way == 0 else (t + step) % nt
        ref = wbuf.at[pl.ds(pl.multiple_of(slot * HD, HD), HD)]
        return remote(ref, ref, w_send.at[way, step], w_recv.at[way, step], right if way == 0 else left)

    def w_step(step):
        for way, count in ((0, rsteps), (1, lsteps)):
            if step >= 1 and step - 1 < count:
                w_copy(way, step - 1).wait_recv()
            if step < count:
                w_copy(way, step).start()

    def w_finish():
        for way, count in ((0, rsteps), (1, lsteps)):
            for step in range(count):
                w_copy(way, step).wait_send()

    def gather(buf, ssem, rsem, pause):
        def hop(uu, du, dv, n):
            src = chip(uu, v)
            return remote(buf.at[src], buf.at[src], ssem.at[n], rsem.at[src], (chip(u + du, v + dv) * 2 + h, t))

        def arrived(src):
            remote(buf.at[src], buf.at[src], ssem.at[0], rsem.at[src], sib).wait_recv()

        sends = [hop(u, d, 0, n) for n, d in enumerate((1, 3, 2))]
        sends += [hop(u, 0, d, 3 + n) for n, d in enumerate((1, 3, 2))]
        for copy in sends:
            copy.start()
        pause(0)
        for m, du in enumerate((1, 3, 2)):
            arrived(chip(u + du, v))
            for n, d in enumerate((1, 3, 2)):
                copy = hop(u + du, 0, d, 6 + 3 * m + n)
                copy.start()
                sends.append(copy)
        pause(1)
        for m, du in enumerate((0, 1, 3, 2)):
            for dv in (1, 3, 2):
                arrived(chip(u + du, v + dv))
            pause(2 + m)
        for copy in sends:
            copy.wait_send()

    def attend(src, start):
        keys = jnp.concatenate([kv[0, src, 0], kv[1, src, 0]], axis=0)
        pieces = []
        for core in range(2):
            block = kv[core, src, 1]
            pieces += [block[n * HD : (n + 1) * HD] for n in range(TOK // HD)]
        values = jnp.concatenate(pieces, axis=1)
        wide = 256
        for n in range(CT // wide):
            cols = slice(n * wide, (n + 1) * wide)
            score = jnp.dot(keys, qt[:, cols], preferred_element_type=F32) * SCALE
            kpos = src * CT + iota((CT, wide), 0)
            visible = kpos >= first[:, cols]
            if start:
                visible = visible & (kpos <= pos[:, cols])
            score = jnp.where(visible, score, FLOOR)
            top = jnp.max(score, axis=0, keepdims=True)
            if not start:
                old = stat[0:1, cols]
                top = jnp.maximum(top, old)
                decay = jnp.exp2(old - top)
            weight = jnp.exp2(score - top)
            total = jnp.sum(weight, axis=0, keepdims=True)
            context = jnp.dot(values, weight.astype(BF), preferred_element_type=F32)
            if not start:
                total = total + stat[1:2, cols] * decay
                context = context + acc[:, cols] * decay
            stat[0:1, cols] = top
            stat[1:2, cols] = total
            acc[:, cols] = context

    def swap_copy(src):
        ref = kv.at[h, src]
        return remote(ref, ref, sib_send.at[src], sib_recv.at[src], sib)

    def swap_wait(src):
        ref = kv.at[1 - h, src]
        remote(ref, ref, sib_send.at[src], sib_recv.at[src], sib).wait_recv()

    q_send = remote(q_hbm.at[:, pl.ds(other_head, HD)], qbuf.at[h], q_sem.at[0], q_sem.at[1], sib)
    q_send.start()

    def kv_copy(src, ssem, to):
        ref = kv.at[h, src]
        return remote(ref, ref, ssem, kv_recv.at[to - src], (to * 2 + h, t))

    own_sends = [(4, y < 3), (8, y < 2), (1, x < 3), (2, x < 2), (3, x < 1)]

    def forwards(dy):
        for dx in range(1, SIDE):
            to = y * SIDE + (x + dx) % SIDE
            yield kv_copy(c - 4 * dy, fwd_send.at[dy - 1, dx - 1], to), (y >= dy) & ((dy == 1) | (x + dx >= SIDE))

    for k, cond in own_sends:

        @pl.when(cond)
        def _():
            kv_copy(c, kv_send.at[k], c + k).start()

    swap_copy(c).start()
    w_step(0)
    q_send.wait_recv()
    for core in range(2):
        rows = qbuf[core].astype(F32).T.astype(BF)
        some = jnp.dot(rows, perm[core * TOK : (core + 1) * TOK, :], preferred_element_type=F32)
        if core == 0:
            total = some
        else:
            total = total + some
    qt[...] = total.astype(BF)
    heard(0)
    hail(1)
    swap_wait(c)
    attend(c, True)

    for dy in (1, 2):

        @pl.when(y >= dy)
        def _():
            kv_copy(c - 4 * dy, kv_send.at[0], c).wait_recv()

        for copy, cond in forwards(dy):

            @pl.when(cond)
            def _():
                copy.start()

    heard(1)
    hail(2)

    reach = jnp.minimum(c, 8)

    @pl.loop(1, reach + 2)
    def _(k):
        @pl.when(k <= reach)
        def _():
            @pl.when(k % 4 > 0)
            def _():
                kv_copy(c - k, kv_send.at[0], c).wait_recv()

            swap_copy(c - k).start()

        @pl.when(k >= 2)
        def _():
            swap_wait(c - k + 1)
            attend(c - k + 1, False)

        for step, at in ((1, 2), (2, 5), (3, 8)):

            @pl.when(k == at)
            def _():
                w_step(step)

    for step, at in ((1, 2), (2, 5), (3, 8)):

        @pl.when(reach + 1 < at)
        def _():
            w_step(step)

    w_step(4)
    result = (acc[...] / stat[1:2, :]).T.astype(BF)
    send1[...] = result

    def a1_copy(d):
        to = (c + d) % CHIPS
        return remote(
            send1.at[pl.ds(pl.multiple_of(to * 32, 32), 32)],
            recv1.at[pl.ds(pl.multiple_of(c * 32, 32), 32)],
            a1_send.at[d],
            a1_recv.at[d],
            (to * 2 + h, t),
        )

    @pl.loop(1, CHIPS)
    def _(d):
        a1_copy(d).start()

    mine = pl.ds(pl.multiple_of(c * 32, 32), 32)
    recv1[mine, :] = send1[mine, :]

    @pl.loop(1, CHIPS)
    def _(d):
        a1_copy(d).wait()


    send2[...] = jnp.dot(perm2[...], recv1[...], preferred_element_type=F32).astype(BF)

    heard(2)

    def z_copy(d):
        to = (t + d) % nt
        return remote(
            send2.at[pl.ds(pl.multiple_of(to * 32, 32), 32)], abuf.at[c, t], z_send.at[d], z_recv.at[d], (me, to)
        )

    @pl.loop(0, nt - 1)
    def _(n):
        z_copy((nt // 2 + (n + 1) // 2 * (1 - 2 * (n % 2))) % nt).start()

    abuf[c, t] = send2[pl.ds(pl.multiple_of(t * 32, 32), 32), :]
    w_step(5)

    @pl.loop(1, nt)
    def _(d):
        z_copy(d).wait()

    half_of = c % 2

    def x_copy(a):
        rows = pl.ds(pl.multiple_of(a * 48, 16), 48)
        return remote(xout.at[rows], xin.at[rows], x_send.at[a], x_recv.at[a], sib)

    def product(chips):
        lhs1 = []
        lhs2 = []
        shared_rows = pl.ds(pl.multiple_of(half_of * 16, 16), 16)
        for s in range(nt):
            lhs1.append(jnp.concatenate([abuf[a, s] for a in chips], axis=0))
            lhs2.append(jnp.concatenate([abuf[a, s, shared_rows, :] for a in chips], axis=0))
        full = jnp.dot(jnp.concatenate(lhs1, axis=1), wbuf[:, 0:256], preferred_element_type=F32)
        some = jnp.dot(jnp.concatenate(lhs2, axis=1), wbuf[:, 256:384], preferred_element_type=F32)
        first_tile = full[:, 0:HD]
        second_tile = full[:, HD:]
        mine = jnp.where(h == 0, first_tile, second_tile)
        other = jnp.where(h == 0, second_tile, first_tile)
        for n, a in enumerate(chips):
            at = pl.multiple_of(a * 48, 16)
            part[pl.ds(at, 32), :] = mine[n * 32 : (n + 1) * 32]
            part[pl.ds(at + 32, 16), :] = some[n * 16 : (n + 1) * 16]
            xout[pl.ds(at, 32), :] = other[n * 32 : (n + 1) * 32]
            xout[pl.ds(at + 32, 16), :] = some[n * 16 : (n + 1) * 16]
            x_copy(a).start()

    def ag_pause(n):
        if n == 0:
            w_step(6)
        if n == 1:
            w_step(7)
            w_step(8)
            w_finish()
        if n >= 2:
            product([chip(u + (0, 1, 3, 2)[n - 2], v + dv) for dv in range(SIDE)])

    gather(abuf, ag_send, ag_recv, ag_pause)

    @pl.loop(0, CHIPS)
    def _(a):
        x_copy(a).wait()

    for n in range(40):
        base = n if n < 32 else 32 + h * 8 + n - 32
        rows = pl.ds(base, 16, stride=48)
        osend[n] = (part[rows, :] + xin[rows, :]).astype(BF)

    def fin_copy(d):
        to = (me + d) % PLANE
        return remote(osend.at[to], obuf.at[me], fin_send.at[d], fin_recv.at[d], (to, t))

    @pl.loop(1, PLANE)
    def _(d):
        fin_copy(d).start()

    base = half_of * 16 + h * 8
    shared = 32 + c // 2

    def fin2_copy(n):
        return remote(
            osend.at[32 + n], obuf.at[shared], fin_send.at[PLANE + n], fin_recv.at[PLANE + c // 2], (base + n, t)
        )

    @pl.loop(0, 8)
    def _(n):
        @pl.when(base + n != me)
        def _():
            fin2_copy(n).start()

    obuf[me] = osend[me]

    @pl.when((me >= base) & (me < base + 8))
    def _():
        obuf[shared] = osend[32 + jnp.clip(me - base, 0, 7)]

    loads[5].wait()
    loads[6].wait()

    @pl.loop(1, PLANE)
    def _(d):
        fin_copy(d).wait()

    @pl.loop(0, 8)
    def _(n):
        @pl.when(base + n != me)
        def _():
            fin2_copy(n).wait_send()

        @pl.when((2 * n + me // 16) * 2 + (me % 16) // 8 != me)
        def _():
            remote(osend.at[0], obuf.at[32 + n], fin_send.at[0], fin_recv.at[PLANE + n], sib).wait_recv()

    q_send.wait_send()

    @pl.loop(0, reach + 1)
    def _(k):
        swap_copy(c - k).wait_send()

    for k, cond in own_sends:

        @pl.when(cond)
        def _():
            kv_copy(c, kv_send.at[k], c + k).wait_send()

    for dy in (1, 2):
        for copy, cond in forwards(dy):

            @pl.when(cond)
            def _():
                copy.wait_send()

    square = jnp.zeros((orows, HD), F32)
    for n in range(40):
        val = obuf[n].astype(F32)
        square = square + val * val
    mean = jnp.sum(square, axis=1, keepdims=True) / (40 * HD)
    factor = lax.rsqrt(mean + 1e-6)
    for n in range(40):
        cols = slice(n * HD, (n + 1) * HD)
        val = obuf[n].astype(F32) * factor * gainv[n : n + 1, :]
        out_ref[:, cols] = (resv[:, cols].astype(F32) + val).astype(BF)


def per_device(queries, keys, values, out_weight, residual, norm_gain, lengths, owner_blocks):
    nt = lax.axis_size("tp")
    docs = lengths.shape[0]
    width = out_weight.shape[1]
    orows = residual.shape[0]
    any_spec = pl.BlockSpec(memory_space=pl.ANY)
    vmem = pltpu.VMEM
    dma = pltpu.SemaphoreType.DMA
    scratch = dict(
        qbuf=vmem((2, TOK, HD), BF),
        vtmp=vmem((TOK, HD), BF),
        kv=vmem((2, CHIPS, 2, TOK, HD), BF),
        qt=vmem((HD, CT), BF),
        acc=vmem((HD, CT), F32),
        stat=vmem((8, CT), F32),
        send1=vmem((CT, HD), BF),
        recv1=vmem((CT, HD), BF),
        perm=vmem((CT, CT), BF),
        perm2=vmem((CT, CT), BF),
        send2=vmem((CT, HD), BF),
        abuf=vmem((CHIPS, nt, 32, HD), BF),
        wbuf=vmem((nt * HD, 3 * HD), BF),
        part=vmem((CHIPS * 48, HD), F32),
        xout=vmem((CHIPS * 48, HD), F32),
        xin=vmem((CHIPS * 48, HD), F32),
        osend=vmem((40, orows, HD), BF),
        obuf=vmem((40, orows, HD), BF),
        resv=vmem((orows, width), BF),
        gainv=vmem((width // HD, HD), F32),
        hail_sem=pltpu.SemaphoreType.REGULAR((3,)),
        loc_sem=dma((7,)),
        q_sem=dma((2,)),
        kv_send=dma((9,)),
        fwd_send=dma((2, 3)),
        kv_recv=dma((9,)),
        sib_send=dma((CHIPS,)),
        sib_recv=dma((CHIPS,)),
        w_send=dma((2, 8)),
        w_recv=dma((2, 8)),
        a1_send=dma((CHIPS,)),
        a1_recv=dma((CHIPS,)),
        z_send=dma((16,)),
        z_recv=dma((16,)),
        ag_send=dma((15,)),
        ag_recv=dma((CHIPS,)),
        x_send=dma((CHIPS,)),
        x_recv=dma((CHIPS,)),
        fin_send=dma((PLANE + 8,)),
        fin_recv=dma((PLANE + 8,)),
    )
    return pl.pallas_call(
        functools.partial(kernel, nt, docs),
        out_shape=jax.ShapeDtypeStruct((orows, width), BF),
        in_specs=[any_spec] * 6
        + [pl.BlockSpec(memory_space=pltpu.SMEM)] * 2,
        out_specs=pl.BlockSpec(memory_space=pltpu.VMEM),
        scratch_shapes=list(scratch.values()),
        compiler_params=pltpu.CompilerParams(
            collective_id=0, has_side_effects=True, vmem_limit_bytes=60 * 1024 * 1024
        ),
        name="attend_project",
    )(
        queries,
        keys,
        values,
        out_weight,
        residual,
        norm_gain.reshape(width // HD, HD),
        lengths,
        owner_blocks.T,
    )


def solution(mesh):
    in_specs = (
        P("ctx", "tp"),
        P("ctx", "tp"),
        P("ctx", "tp"),
        P("tp", None),
        P(("ctx", "tp"), None),
        P(),
        P(),
        P(),
    )
    out_specs = P(("ctx", "tp"), None)
    return jax.shard_map(
        per_device, mesh=mesh, in_specs=in_specs, out_specs=out_specs, check_vma=False
    )
```

time: 99 us -> 89.7 us (0.906)
  local copies, waits for them, and re-layouts: 8.05 us -> 1.59 us
  Pallas kernels: 90.6 us -> 87.9 us
    unnamed x16 -> x1, local copies, waits for them, and re-layouts: 8.05 us -> 1.59 us
    pallas_call x1, Pallas kernels: 90.6 us -> 87.9 us  [per_device(): pl.pallas_call(functools.partial(kernel, nt, docs), out_shape=jax.ShapeDt...]
where the time goes in v2:
time: 89.7 us; the launch traced here: 89.5 us
  Pallas kernels  87.9 us (98%)
  local copies, waits for them, and re-layouts  1.59 us (2%)
    pallas_call x1, Pallas kernels, per_device(): pl.pallas_call(functools.partial(kernel, nt, docs), out_shape=jax.ShapeDt...  87.9 us

profile of v2, /device:TPU:1, one launch (start us, length us, event | category | flops | bytes accessed | tf_op | source)
XLA Modules:
  0.0 89.5 jit_solution(15346572632836930426)
XLA Ops:
  0.0 87.9 %attend_project.1 = bf16[16,5120]{1,0:T(8,128)(2,1)} custom-call(bf16[256,256]{1,0:T(8,128)(2,1)} %q_hbm.1, bf16[256,128]{1,0:T(8,128)(2,1)} %k_hbm.1, bf16[256,128]{1,0:T(8,128)(2,1)} %v_hbm.1, bf16[256,5120]{1,0:T(8,128)(2,1)} %w_hbm.1, bf16[16,5120]{1,0:T(8,128)(2,1)} %res_hbm.1, f32[40,128]{1,0:T(8,128)} %bitcast.2, s32[32]{0:T(128)} %len_ref.1, ...), custom_call_target="tpu_custom_call" | custom-call | tf_op jit(solution)/shard_map/attend_project/pallas_call | solution.py:557
  87.9 1.6 %copy.10 = bf16[16,5120]{1,0:T(8,128)(2,1)} copy(bf16[16,5120]{1,0:T(8,128)(2,1)} %attend_project.1) | data formatting | bytes 327680

commit v3 on v2

--- a/solution.py
+++ b/solution.py
@@ -17,6 +17,8 @@
 CHIPS = SIDE * SIDE
 CT = 2 * TOK
 PLANE = 2 * CHIPS
+TILES = 5
+WIDE = TILES * HD
 FLOOR = -1e30
 SCALE = math.log2(math.e) / math.sqrt(HD)
 BF = jnp.bfloat16
@@ -53,10 +55,10 @@
     abuf,
     wbuf,
     part,
-    xout,
-    xin,
     osend,
     obuf,
+    pick,
+    proj,
     resv,
     gainv,
     hail_sem,
@@ -69,14 +71,14 @@
     sib_recv,
     w_send,
     w_recv,
+    wv_send,
+    wv_recv,
     a1_send,
     a1_recv,
     z_send,
     z_recv,
     ag_send,
     ag_recv,
-    x_send,
-    x_recv,
     fin_send,
     fin_recv,
 ):
@@ -101,15 +103,15 @@
 
     head = pl.multiple_of(h * HD, HD)
     other_head = pl.multiple_of((1 - h) * HD, HD)
-    my_w = pl.ds(pl.multiple_of(t * HD, HD), HD)
-    col1 = pl.ds(pl.multiple_of(c * 256, 256), 256)
-    col2 = pl.ds(pl.multiple_of(4096 + (c // 2) * 128, 128), 128)
+    HERE = nt // 4
+    low, high = v % 2, v // 2
+    w_rows = pl.ds(pl.multiple_of(h * HD + low * 64, 64), 64)
+    w_cols = pl.ds(pl.multiple_of((u * 2 + high) * WIDE, HD), WIDE)
     loads = [
         (k_hbm, kv.at[h, c, 0]),
         (v_hbm, vtmp),
         (q_hbm.at[:, pl.ds(head, HD)], qbuf.at[h]),
-        (w_hbm.at[pl.ds(head, HD), col1], wbuf.at[my_w, pl.ds(0, 256)]),
-        (w_hbm.at[pl.ds(head, HD), col2], wbuf.at[my_w, pl.ds(256, 128)]),
+        (w_hbm.at[w_rows, w_cols], wbuf.at[HERE, low]),
         (res_hbm, resv),
         (gain_hbm, gainv),
     ]
@@ -147,6 +149,18 @@
             rows = slice((k * 8 + i) * PLANE, (k * 8 + i + 1) * PLANE)
             perm2[rows, :] = jnp.where(iota((PLANE, CT), 1) == owned + i, 1.0, 0.0).astype(BF)
 
+    row = iota((TILES * 16, 1), 0)
+    tile_of = row // 16
+    chip_of = row % 16
+    lane = iota((TILES * 16, 192), 1)
+
+    def place(uu, vv):
+        return (vv % 2) * 48 + tile_of * 8 + (vv // 2) * 4 + uu
+
+    picked = (lane == place(chip_of % 4, chip_of // 4)) | (lane == 96 + place(chip_of // 4, chip_of % 4))
+    pick[...] = jnp.where(picked, 1.0, 0.0).astype(BF)
+    part[2 * WIDE :, :] = jnp.zeros((256, HD), F32)
+
     loads[0].wait()
     loads[1].wait()
     vt = vtmp[...].astype(F32)
@@ -154,7 +168,6 @@
         kv[h, c, 1, n * HD : (n + 1) * HD, :] = vt[n * HD : (n + 1) * HD, :].T.astype(BF)
     loads[2].wait()
     loads[3].wait()
-    loads[4].wait()
 
     pl.semaphore_wait(barrier, CHIPS + 2)
 
@@ -171,9 +184,14 @@
     lsteps = nt - 1 - rsteps
 
     def w_copy(way, step):
-        slot = (t - step + nt) % nt if way == 0 else (t + step) % nt
-        ref = wbuf.at[pl.ds(pl.multiple_of(slot * HD, HD), HD)]
-        return remote(ref, ref, w_send.at[way, step], w_recv.at[way, step], right if way == 0 else left)
+        sign = 1 if way else -1
+        src = wbuf.at[(HERE + sign * step) % nt, low]
+        dst = wbuf.at[(HERE + sign * (step + 1)) % nt, low]
+        return remote(src, dst, w_send.at[way, step], w_recv.at[way, step], left if way else right)
+
+    def w_spread(slot):
+        ref = wbuf.at[slot, low]
+        return remote(ref, ref, wv_send.at[slot], wv_recv.at[slot], (chip(u, v + 1 - 2 * low) * 2 + h, t))
 
     def w_step(step):
         for way, count in ((0, rsteps), (1, lsteps)):
@@ -182,37 +200,22 @@
             if step < count:
                 w_copy(way, step).start()
 
+    def w_share(step):
+        for way, count in ((0, rsteps), (1, lsteps)):
+            if (step >= 1 and step - 1 < count) or (step == 0 and way == 0):
+                w_spread((HERE + (1 if way else -1) * step) % nt).start()
+
     def w_finish():
         for way, count in ((0, rsteps), (1, lsteps)):
             for step in range(count):
                 w_copy(way, step).wait_send()
-
-    def gather(buf, ssem, rsem, pause):
-        def hop(uu, du, dv, n):
-            src = chip(uu, v)
-            return remote(buf.at[src], buf.at[src], ssem.at[n], rsem.at[src], (chip(u + du, v + dv) * 2 + h, t))
-
-        def arrived(src):
-            remote(buf.at[src], buf.at[src], ssem.at[0], rsem.at[src], sib).wait_recv()
-
-        sends = [hop(u, d, 0, n) for n, d in enumerate((1, 3, 2))]
-        sends += [hop(u, 0, d, 3 + n) for n, d in enumerate((1, 3, 2))]
-        for copy in sends:
-            copy.start()
-        pause(0)
-        for m, du in enumerate((1, 3, 2)):
-            arrived(chip(u + du, v))
-            for n, d in enumerate((1, 3, 2)):
-                copy = hop(u + du, 0, d, 6 + 3 * m + n)
-                copy.start()
-                sends.append(copy)
-        pause(1)
-        for m, du in enumerate((0, 1, 3, 2)):
-            for dv in (1, 3, 2):
-                arrived(chip(u + du, v + dv))
-            pause(2 + m)
-        for copy in sends:
-            copy.wait_send()
+        for slot in range(nt):
+            w_spread(slot).wait_send()
+
+    def w_arrived(slots):
+        for slot in slots:
+            ref = wbuf.at[slot, 1 - low]
+            remote(ref, ref, wv_send.at[slot], wv_recv.at[slot], sib).wait_recv()
 
     def attend(src, start):
         keys = jnp.concatenate([kv[0, src, 0], kv[1, src, 0]], axis=0)
@@ -289,6 +292,8 @@
     swap_wait(c)
     attend(c, True)
 
+    w_step(1)
+
     for dy in (1, 2):
 
         @pl.when(y >= dy)
@@ -301,6 +306,8 @@
             def _():
                 copy.start()
 
+    w_share(0)
+    w_share(1)
     heard(1)
     hail(2)
 
@@ -321,17 +328,19 @@
             swap_wait(c - k + 1)
             attend(c - k + 1, False)
 
-        for step, at in ((1, 2), (2, 5), (3, 8)):
+        for step, at in ((2, 4), (3, 7)):
 
             @pl.when(k == at)
             def _():
                 w_step(step)
-
-    for step, at in ((1, 2), (2, 5), (3, 8)):
+                w_share(step)
+
+    for step, at in ((2, 4), (3, 7)):
 
         @pl.when(reach + 1 < at)
         def _():
             w_step(step)
+            w_share(step)
 
     w_step(4)
     result = (acc[...] / stat[1:2, :]).T.astype(BF)
@@ -347,10 +356,16 @@
             (to * 2 + h, t),
         )
 
-    @pl.loop(1, CHIPS)
-    def _(d):
-        a1_copy(d).start()
-
+    def outward(n, size):
+        return (size // 2 + (n + 1) // 2 * (1 - 2 * (n % 2))) % size
+
+    @pl.loop(0, CHIPS - 1)
+    def _(n):
+        a1_copy(outward(n, CHIPS)).start()
+
+    w_share(4)
+    w_step(5)
+    w_share(5)
     mine = pl.ds(pl.multiple_of(c * 32, 32), 32)
     recv1[mine, :] = send1[mine, :]
 
@@ -366,141 +381,144 @@
     def z_copy(d):
         to = (t + d) % nt
         return remote(
-            send2.at[pl.ds(pl.multiple_of(to * 32, 32), 32)], abuf.at[c, t], z_send.at[d], z_recv.at[d], (me, to)
+            send2.at[pl.ds(pl.multiple_of(to * 32, 32), 32)],
+            abuf.at[high, u, (HERE - d + nt) % nt],
+            z_send.at[d],
+            z_recv.at[d],
+            (me, to),
         )
 
     @pl.loop(0, nt - 1)
     def _(n):
-        z_copy((nt // 2 + (n + 1) // 2 * (1 - 2 * (n % 2))) % nt).start()
-
-    abuf[c, t] = send2[pl.ds(pl.multiple_of(t * 32, 32), 32), :]
-    w_step(5)
+        z_copy(outward(n, nt)).start()
+
+    abuf[high, u, HERE] = send2[pl.ds(pl.multiple_of(t * 32, 32), 32), :]
+    w_step(6)
+    w_share(6)
+
+    lower = nt // 2
+
+    def ag_copy(own, du, side):
+        at = high if own == 0 else 1 - high
+        ref = abuf.at[at, u, pl.ds(side * lower, lower)]
+        to = chip(u, v + 2) if du == 0 else chip(u + du, v)
+        return remote(ref, ref, ag_send.at[own, side, du], ag_recv.at[at, u, side], (to * 2 + h, t))
+
+    def ag_arrived(own, du, side):
+        at = high if own == 0 else 1 - high
+        uu = (u + du) % SIDE
+        ref = abuf.at[at, uu, pl.ds(side * lower, lower)]
+        remote(ref, ref, ag_send.at[0, 0, 0], ag_recv.at[at, uu, side], sib).wait_recv()
+
+    def ag_all(side):
+        for own in (0, 1):
+            for du in (1, 3, 2):
+                ag_arrived(own, du, side)
+
+    def ag_onward(side):
+        ag_arrived(1, 0, side)
+        for du in (2, 1, 3):
+            ag_copy(1, du, side).start()
+
+    def product(side):
+        lhs = [abuf[:, :, side * lower + n].reshape(2 * SIDE * 32, HD) for n in range(lower)]
+        lhs = jnp.concatenate(lhs, axis=1)
+        for first_tile in range(0, TILES, 2):
+            tiles = min(2, TILES - first_tile)
+            rhs = wbuf[side * lower : (side + 1) * lower, :, :, first_tile * HD : (first_tile + tiles) * HD]
+            val = jnp.dot(lhs, rhs.reshape(lower * HD, tiles * HD), preferred_element_type=F32)
+            for m in range(tiles):
+                rows = slice((first_tile + m) * 256, (first_tile + m + 1) * 256)
+                piece = val[:, m * HD : (m + 1) * HD]
+                part[rows, :] = piece if side == 0 else part[rows, :] + piece
 
     @pl.loop(1, nt)
     def _(d):
-        z_copy(d).wait()
-
-    half_of = c % 2
-
-    def x_copy(a):
-        rows = pl.ds(pl.multiple_of(a * 48, 16), 48)
-        return remote(xout.at[rows], xin.at[rows], x_send.at[a], x_recv.at[a], sib)
-
-    def product(chips):
-        lhs1 = []
-        lhs2 = []
-        shared_rows = pl.ds(pl.multiple_of(half_of * 16, 16), 16)
-        for s in range(nt):
-            lhs1.append(jnp.concatenate([abuf[a, s] for a in chips], axis=0))
-            lhs2.append(jnp.concatenate([abuf[a, s, shared_rows, :] for a in chips], axis=0))
-        full = jnp.dot(jnp.concatenate(lhs1, axis=1), wbuf[:, 0:256], preferred_element_type=F32)
-        some = jnp.dot(jnp.concatenate(lhs2, axis=1), wbuf[:, 256:384], preferred_element_type=F32)
-        first_tile = full[:, 0:HD]
-        second_tile = full[:, HD:]
-        mine = jnp.where(h == 0, first_tile, second_tile)
-        other = jnp.where(h == 0, second_tile, first_tile)
-        for n, a in enumerate(chips):
-            at = pl.multiple_of(a * 48, 16)
-            part[pl.ds(at, 32), :] = mine[n * 32 : (n + 1) * 32]
-            part[pl.ds(at + 32, 16), :] = some[n * 16 : (n + 1) * 16]
-            xout[pl.ds(at, 32), :] = other[n * 32 : (n + 1) * 32]
-            xout[pl.ds(at + 32, 16), :] = some[n * 16 : (n + 1) * 16]
-            x_copy(a).start()
-
-    def ag_pause(n):
-        if n == 0:
-            w_step(6)
-        if n == 1:
-            w_step(7)
-            w_step(8)
-            w_finish()
-        if n >= 2:
-            product([chip(u + (0, 1, 3, 2)[n - 2], v + dv) for dv in range(SIDE)])
-
-    gather(abuf, ag_send, ag_recv, ag_pause)
-
-    @pl.loop(0, CHIPS)
-    def _(a):
-        x_copy(a).wait()
-
-    for n in range(40):
-        base = n if n < 32 else 32 + h * 8 + n - 32
-        rows = pl.ds(base, 16, stride=48)
-        osend[n] = (part[rows, :] + xin[rows, :]).astype(BF)
+        @pl.when((d <= HERE) | (d > nt - HERE))
+        def _():
+            z_copy(d).wait()
+
+    for du in (0, 2, 1, 3):
+        ag_copy(0, du, 0).start()
+    w_step(7)
+    w_share(7)
+
+    @pl.loop(1, nt)
+    def _(d):
+        @pl.when((d > HERE) & (d <= nt - HERE))
+        def _():
+            z_copy(d).wait()
+
+    for du in (0, 2, 1, 3):
+        ag_copy(0, du, 1).start()
+    ag_onward(0)
+    w_step(8)
+    w_share(8)
+    ag_onward(1)
+    ag_all(0)
+    w_arrived(range(lower))
+    product(0)
+    ag_all(1)
+    w_arrived(range(lower, nt))
+    product(1)
+
+    for o in range(PLANE):
+        osend[o] = part[pl.ds(o, 48, stride=32), :].astype(BF)
+
+    mine = (h * SIDE + u) * SIDE + v
 
     def fin_copy(d):
         to = (me + d) % PLANE
-        return remote(osend.at[to], obuf.at[me], fin_send.at[d], fin_recv.at[d], (to, t))
+        return remote(osend.at[to], obuf.at[mine], fin_send.at[d], fin_recv.at[d], (to, t))
 
     @pl.loop(1, PLANE)
     def _(d):
-        fin_copy(d).start()
-
-    base = half_of * 16 + h * 8
-    shared = 32 + c // 2
-
-    def fin2_copy(n):
-        return remote(
-            osend.at[32 + n], obuf.at[shared], fin_send.at[PLANE + n], fin_recv.at[PLANE + c // 2], (base + n, t)
-        )
-
-    @pl.loop(0, 8)
-    def _(n):
-        @pl.when(base + n != me)
-        def _():
-            fin2_copy(n).start()
-
-    obuf[me] = osend[me]
-
-    @pl.when((me >= base) & (me < base + 8))
-    def _():
-        obuf[shared] = osend[32 + jnp.clip(me - base, 0, 7)]
-
+        fin_copy(outward(d - 1, PLANE)).start()
+
+    obuf[mine] = osend[me]
+    loads[4].wait()
     loads[5].wait()
-    loads[6].wait()
+    w_finish()
+    for own, du in ((0, 0), (0, 1), (0, 2), (0, 3), (1, 1), (1, 2), (1, 3)):
+        for side in range(2):
+            ag_copy(own, du, side).wait_send()
+
+    q_send.wait_send()
+
+    @pl.loop(0, reach + 1)
+    def _(k):
+        swap_copy(c - k).wait_send()
+
+    for k, cond in own_sends:
+
+        @pl.when(cond)
+        def _():
+            kv_copy(c, kv_send.at[k], c + k).wait_send()
+
+    for dy in (1, 2):
+        for copy, cond in forwards(dy):
+
+            @pl.when(cond)
+            def _():
+                copy.wait_send()
 
     @pl.loop(1, PLANE)
     def _(d):
         fin_copy(d).wait()
 
-    @pl.loop(0, 8)
-    def _(n):
-        @pl.when(base + n != me)
-        def _():
-            fin2_copy(n).wait_send()
-
-        @pl.when((2 * n + me // 16) * 2 + (me % 16) // 8 != me)
-        def _():
-            remote(osend.at[0], obuf.at[32 + n], fin_send.at[0], fin_recv.at[PLANE + n], sib).wait_recv()
-
-    q_send.wait_send()
-
-    @pl.loop(0, reach + 1)
-    def _(k):
-        swap_copy(c - k).wait_send()
-
-    for k, cond in own_sends:
-
-        @pl.when(cond)
-        def _():
-            kv_copy(c, kv_send.at[k], c + k).wait_send()
-
-    for dy in (1, 2):
-        for copy, cond in forwards(dy):
-
-            @pl.when(cond)
-            def _():
-                copy.wait_send()
-
     square = jnp.zeros((orows, HD), F32)
-    for n in range(40):
-        val = obuf[n].astype(F32)
-        square = square + val * val
-    mean = jnp.sum(square, axis=1, keepdims=True) / (40 * HD)
+    for g in range(2 * SIDE):
+        both = [obuf[core * 16 + g * 2 + n] for core in range(2) for n in range(2)]
+        total = jnp.dot(pick[...], jnp.concatenate(both, axis=0), preferred_element_type=F32)
+        proj[g * TILES * 16 : (g + 1) * TILES * 16, :] = total
+        for j in range(TILES):
+            val = total[j * 16 : (j + 1) * 16]
+            square = square + val * val
+    mean = jnp.sum(square, axis=1, keepdims=True) / (8 * WIDE)
     factor = lax.rsqrt(mean + 1e-6)
-    for n in range(40):
+    for n in range(8 * TILES):
         cols = slice(n * HD, (n + 1) * HD)
-        val = obuf[n].astype(F32) * factor * gainv[n : n + 1, :]
+        val = proj[n * 16 : (n + 1) * 16, :] * factor * gainv[n : n + 1, :]
         out_ref[:, cols] = (resv[:, cols].astype(F32) + val).astype(BF)
 
 
@@ -524,17 +542,17 @@
         perm=vmem((CT, CT), BF),
         perm2=vmem((CT, CT), BF),
         send2=vmem((CT, HD), BF),
-        abuf=vmem((CHIPS, nt, 32, HD), BF),
-        wbuf=vmem((nt * HD, 3 * HD), BF),
-        part=vmem((CHIPS * 48, HD), F32),
-        xout=vmem((CHIPS * 48, HD), F32),
-        xin=vmem((CHIPS * 48, HD), F32),
-        osend=vmem((40, orows, HD), BF),
-        obuf=vmem((40, orows, HD), BF),
+        abuf=vmem((2, SIDE, nt, 32, HD), BF),
+        wbuf=vmem((nt, 2, 64, WIDE), BF),
+        part=vmem((2 * WIDE + 256, HD), F32),
+        osend=vmem((PLANE, 48, HD), BF),
+        obuf=vmem((PLANE, 48, HD), BF),
+        pick=vmem((TILES * 16, 192), BF),
+        proj=vmem((8 * TILES * 16, HD), F32),
         resv=vmem((orows, width), BF),
         gainv=vmem((width // HD, HD), F32),
         hail_sem=pltpu.SemaphoreType.REGULAR((3,)),
-        loc_sem=dma((7,)),
+        loc_sem=dma((6,)),
         q_sem=dma((2,)),
         kv_send=dma((9,)),
         fwd_send=dma((2, 3)),
@@ -543,16 +561,16 @@
         sib_recv=dma((CHIPS,)),
         w_send=dma((2, 8)),
         w_recv=dma((2, 8)),
+        wv_send=dma((16,)),
+        wv_recv=dma((16,)),
         a1_send=dma((CHIPS,)),
         a1_recv=dma((CHIPS,)),
         z_send=dma((16,)),
         z_recv=dma((16,)),
-        ag_send=dma((15,)),
-        ag_recv=dma((CHIPS,)),
-        x_send=dma((CHIPS,)),
-        x_recv=dma((CHIPS,)),
-        fin_send=dma((PLANE + 8,)),
-        fin_recv=dma((PLANE + 8,)),
+        ag_send=dma((2, 2, SIDE)),
+        ag_recv=dma((2, SIDE, 2)),
+        fin_send=dma((PLANE,)),
+        fin_recv=dma((PLANE,)),
     )
     return pl.pallas_call(
         functools.partial(kernel, nt, docs),

time: 89.7 us -> 81.9 us (0.913)
  Pallas kernels: 87.9 us -> 80.2 us
    pallas_call x1, Pallas kernels: 87.9 us -> 80.2 us  [per_device(): pl.pallas_call(functools.partial(kernel, nt, docs), out_shape=jax.ShapeDt...]
where the time goes in v3:
time: 81.9 us; the launch traced here: 81.8 us
  Pallas kernels  80.2 us (98%)
  local copies, waits for them, and re-layouts  1.59 us (2%)
    pallas_call x1, Pallas kernels, per_device(): pl.pallas_call(functools.partial(kernel, nt, docs), out_shape=jax.ShapeDt...  80.2 us

profile of v3, /device:TPU:1, one launch (start us, length us, event | category | flops | bytes accessed | tf_op | source)
XLA Modules:
  0.0 81.8 jit_solution(2099343343875436258)
XLA Ops:
  0.0 80.2 %attend_project.1 = bf16[16,5120]{1,0:T(8,128)(2,1)} custom-call(bf16[256,256]{1,0:T(8,128)(2,1)} %q_hbm.1, bf16[256,128]{1,0:T(8,128)(2,1)} %k_hbm.1, bf16[256,128]{1,0:T(8,128)(2,1)} %v_hbm.1, bf16[256,5120]{1,0:T(8,128)(2,1)} %w_hbm.1, bf16[16,5120]{1,0:T(8,128)(2,1)} %res_hbm.1, f32[40,128]{1,0:T(8,128)} %bitcast.2, s32[32]{0:T(128)} %len_ref.1, ...), custom_call_target="tpu_custom_call" | custom-call | tf_op jit(solution)/shard_map/attend_project/pallas_call | solution.py:575
  80.2 1.6 %copy.10 = bf16[16,5120]{1,0:T(8,128)(2,1)} copy(bf16[16,5120]{1,0:T(8,128)(2,1)} %attend_project.1) | data formatting | bytes 327680

commit v4 on v3

--- a/solution.py
+++ b/solution.py
@@ -311,38 +311,35 @@
     heard(1)
     hail(2)
 
-    reach = jnp.minimum(c, 8)
-
-    @pl.loop(1, reach + 2)
-    def _(k):
-        @pl.when(k <= reach)
+    def back(i):
+        return jnp.where(i == 1, 4, jnp.where(i == 2, 8, jnp.where(i < 6, i - 2, i - 1)))
+
+    @pl.loop(1, 10)
+    def _(i):
+        k = back(i)
+
+        @pl.when((i < 9) & (k <= c))
         def _():
-            @pl.when(k % 4 > 0)
+            @pl.when(i > 2)
             def _():
                 kv_copy(c - k, kv_send.at[0], c).wait_recv()
 
             swap_copy(c - k).start()
 
-        @pl.when(k >= 2)
-        def _():
-            swap_wait(c - k + 1)
-            attend(c - k + 1, False)
-
-        for step, at in ((2, 4), (3, 7)):
-
-            @pl.when(k == at)
+        for step, at in ((2, 5), (3, 8)):
+
+            @pl.when(i == at)
             def _():
                 w_step(step)
                 w_share(step)
 
-    for step, at in ((2, 4), (3, 7)):
-
-        @pl.when(reach + 1 < at)
+        before = back(i - 1)
+
+        @pl.when((i >= 2) & (before <= c))
         def _():
-            w_step(step)
-            w_share(step)
-
-    w_step(4)
+            swap_wait(c - before)
+            attend(c - before, False)
+
     result = (acc[...] / stat[1:2, :]).T.astype(BF)
     send1[...] = result
 
@@ -363,6 +360,7 @@
     def _(n):
         a1_copy(outward(n, CHIPS)).start()
 
+    w_step(4)
     w_share(4)
     w_step(5)
     w_share(5)
@@ -485,7 +483,7 @@
 
     q_send.wait_send()
 
-    @pl.loop(0, reach + 1)
+    @pl.loop(0, jnp.minimum(c, 8) + 1)
     def _(k):
         swap_copy(c - k).wait_send()
 

time: 81.9 us -> 78.3 us (0.956)
  Pallas kernels: 80.2 us -> 76.6 us
    pallas_call x1, Pallas kernels: 80.2 us -> 76.6 us  [per_device(): pl.pallas_call(functools.partial(kernel, nt, docs), out_shape=jax.ShapeDt...]
where the time goes in v4:
time: 78.3 us; the launch traced here: 78.2 us
  Pallas kernels  76.6 us (98%)
  local copies, waits for them, and re-layouts  1.59 us (2%)
    pallas_call x1, Pallas kernels, per_device(): pl.pallas_call(functools.partial(kernel, nt, docs), out_shape=jax.ShapeDt...  76.6 us
    unnamed x1, local copies, waits for them, and re-layouts  1.59 us

profile of v4, /device:TPU:1, one launch (start us, length us, event | category | flops | bytes accessed | tf_op | source)
XLA Modules:
  0.0 78.2 jit_solution(4437411896954821282)
XLA Ops:
  0.0 76.6 %attend_project.1 = bf16[16,5120]{1,0:T(8,128)(2,1)} custom-call(bf16[256,256]{1,0:T(8,128)(2,1)} %q_hbm.1, bf16[256,128]{1,0:T(8,128)(2,1)} %k_hbm.1, bf16[256,128]{1,0:T(8,128)(2,1)} %v_hbm.1, bf16[256,5120]{1,0:T(8,128)(2,1)} %w_hbm.1, bf16[16,5120]{1,0:T(8,128)(2,1)} %res_hbm.1, f32[40,128]{1,0:T(8,128)} %bitcast.2, s32[32]{0:T(128)} %len_ref.1, ...), custom_call_target="tpu_custom_call" | custom-call | tf_op jit(solution)/shard_map/attend_project/pallas_call | solution.py:573
  76.6 1.6 %copy.10 = bf16[16,5120]{1,0:T(8,128)(2,1)} copy(bf16[16,5120]{1,0:T(8,128)(2,1)} %attend_project.1) | data formatting | bytes 327680

commit v5 on v4

--- a/solution.py
+++ b/solution.py
@@ -38,9 +38,11 @@
     w_hbm,
     res_hbm,
     gain_hbm,
+    len_hbm,
+    own_hbm,
+    out_ref,
     len_ref,
     own_ref,
-    out_ref,
     qbuf,
     vtmp,
     kv,
@@ -114,6 +116,8 @@
         (w_hbm.at[w_rows, w_cols], wbuf.at[HERE, low]),
         (res_hbm, resv),
         (gain_hbm, gainv),
+        (len_hbm, len_ref),
+        (own_hbm, own_ref),
     ]
     loads = [pltpu.make_async_copy(s, d, loc_sem.at[n]) for n, (s, d) in enumerate(loads)]
     for copy in loads:
@@ -137,6 +141,8 @@
     pos = c * CT + ((lane // 8) % 4) * BLOCK + (lane % 8) * 16 + lane // 32
     first = jnp.zeros((1, CT), jnp.int32)
     end = jnp.int32(0)
+    loads[6].wait()
+    loads[7].wait()
     for n in range(docs):
         end = end + len_ref[n]
         first = jnp.where(end <= pos, end, first)
@@ -259,22 +265,23 @@
     q_send = remote(q_hbm.at[:, pl.ds(other_head, HD)], qbuf.at[h], q_sem.at[0], q_sem.at[1], sib)
     q_send.start()
 
-    def kv_copy(src, ssem, to):
-        ref = kv.at[h, src]
-        return remote(ref, ref, ssem, kv_recv.at[to - src], (to * 2 + h, t))
+    def kv_copy(src, ssem, to, part):
+        ref = kv.at[h, src, part]
+        return remote(ref, ref, ssem, kv_recv.at[to - src, part], (to * 2 + h, t))
 
     own_sends = [(4, y < 3), (8, y < 2), (1, x < 3), (2, x < 2), (3, x < 1)]
 
-    def forwards(dy):
+    def forwards(dy, part):
         for dx in range(1, SIDE):
             to = y * SIDE + (x + dx) % SIDE
-            yield kv_copy(c - 4 * dy, fwd_send.at[dy - 1, dx - 1], to), (y >= dy) & ((dy == 1) | (x + dx >= SIDE))
+            yield kv_copy(c - 4 * dy, fwd_send.at[dy - 1, dx - 1, part], to, part), (y >= dy) & ((dy == 1) | (x + dx >= SIDE))
 
     for k, cond in own_sends:
 
         @pl.when(cond)
         def _():
-            kv_copy(c, kv_send.at[k], c + k).start()
+            for side in range(2):
+                kv_copy(c, kv_send.at[k, side], c + k, side).start()
 
     swap_copy(c).start()
     w_step(0)
@@ -294,13 +301,13 @@
 
     w_step(1)
 
-    for dy in (1, 2):
+    for dy, side in ((1, 0), (1, 1), (2, 0), (2, 1)):
 
         @pl.when(y >= dy)
         def _():
-            kv_copy(c - 4 * dy, kv_send.at[0], c).wait_recv()
-
-        for copy, cond in forwards(dy):
+            kv_copy(c - 4 * dy, kv_send.at[0, 0], c, side).wait_recv()
+
+        for copy, cond in forwards(dy, side):
 
             @pl.when(cond)
             def _():
@@ -322,7 +329,8 @@
         def _():
             @pl.when(i > 2)
             def _():
-                kv_copy(c - k, kv_send.at[0], c).wait_recv()
+                for side in range(2):
+                    kv_copy(c - k, kv_send.at[0, 0], c, side).wait_recv()
 
             swap_copy(c - k).start()
 
@@ -460,20 +468,22 @@
     w_arrived(range(lower, nt))
     product(1)
 
-    for o in range(PLANE):
-        osend[o] = part[pl.ds(o, 48, stride=32), :].astype(BF)
-
     mine = (h * SIDE + u) * SIDE + v
 
     def fin_copy(d):
         to = (me + d) % PLANE
         return remote(osend.at[to], obuf.at[mine], fin_send.at[d], fin_recv.at[d], (to, t))
 
+    def pack(o):
+        return part[pl.ds(o, 48, stride=32), :].astype(BF)
+
     @pl.loop(1, PLANE)
-    def _(d):
-        fin_copy(outward(d - 1, PLANE)).start()
-
-    obuf[mine] = osend[me]
+    def _(n):
+        d = outward(n - 1, PLANE)
+        osend[(me + d) % PLANE] = pack((me + d) % PLANE)
+        fin_copy(d).start()
+
+    obuf[mine] = pack(me)
     loads[4].wait()
     loads[5].wait()
     w_finish()
@@ -491,10 +501,11 @@
 
         @pl.when(cond)
         def _():
-            kv_copy(c, kv_send.at[k], c + k).wait_send()
-
-    for dy in (1, 2):
-        for copy, cond in forwards(dy):
+            for side in range(2):
+                kv_copy(c, kv_send.at[k, side], c + k, side).wait_send()
+
+    for dy, side in ((1, 0), (1, 1), (2, 0), (2, 1)):
+        for copy, cond in forwards(dy, side):
 
             @pl.when(cond)
             def _():
@@ -529,6 +540,8 @@
     vmem = pltpu.VMEM
     dma = pltpu.SemaphoreType.DMA
     scratch = dict(
+        len_ref=pltpu.SMEM((docs,), jnp.int32),
+        own_ref=pltpu.SMEM((2, PLANE), jnp.int32),
         qbuf=vmem((2, TOK, HD), BF),
         vtmp=vmem((TOK, HD), BF),
         kv=vmem((2, CHIPS, 2, TOK, HD), BF),
@@ -550,11 +563,11 @@
         resv=vmem((orows, width), BF),
         gainv=vmem((width // HD, HD), F32),
         hail_sem=pltpu.SemaphoreType.REGULAR((3,)),
-        loc_sem=dma((6,)),
+        loc_sem=dma((8,)),
         q_sem=dma((2,)),
-        kv_send=dma((9,)),
-        fwd_send=dma((2, 3)),
-        kv_recv=dma((9,)),
+        kv_send=dma((9, 2)),
+        fwd_send=dma((2, 3, 2)),
+        kv_recv=dma((9, 2)),
         sib_send=dma((CHIPS,)),
         sib_recv=dma((CHIPS,)),
         w_send=dma((2, 8)),
@@ -573,8 +586,7 @@
     return pl.pallas_call(
         functools.partial(kernel, nt, docs),
         out_shape=jax.ShapeDtypeStruct((orows, width), BF),
-        in_specs=[any_spec] * 6
-        + [pl.BlockSpec(memory_space=pltpu.SMEM)] * 2,
+        in_specs=[any_spec] * 8,
         out_specs=pl.BlockSpec(memory_space=pltpu.VMEM),
         scratch_shapes=list(scratch.values()),
         compiler_params=pltpu.CompilerParams(

time: 78.3 us -> 77 us (0.983)
  Pallas kernels: 76.6 us -> 75.2 us
    pallas_call x1, Pallas kernels: 76.6 us -> 75.2 us  [per_device(): pl.pallas_call(functools.partial(kernel, nt, docs), out_shape=jax.ShapeDt...]
where the time goes in v5:
time: 77 us; the launch traced here: 76.8 us
  Pallas kernels  75.2 us (98%)
  local copies, waits for them, and re-layouts  1.59 us (2%)
    pallas_call x1, Pallas kernels, per_device(): pl.pallas_call(functools.partial(kernel, nt, docs), out_shape=jax.ShapeDt...  75.2 us
    unnamed x1, local copies, waits for them, and re-layouts  1.59 us

profile of v5, /device:TPU:1, one launch (start us, length us, event | category | flops | bytes accessed | tf_op | source)
XLA Modules:
  0.0 76.8 jit_solution(16106066108529588719)
XLA Ops:
  0.0 75.2 %attend_project.1 = bf16[16,5120]{1,0:T(8,128)(2,1)} custom-call(bf16[256,256]{1,0:T(8,128)(2,1)} %q_hbm.1, bf16[256,128]{1,0:T(8,128)(2,1)} %k_hbm.1, bf16[256,128]{1,0:T(8,128)(2,1)} %v_hbm.1, bf16[256,5120]{1,0:T(8,128)(2,1)} %w_hbm.1, bf16[16,5120]{1,0:T(8,128)(2,1)} %res_hbm.1, f32[40,128]{1,0:T(8,128)} %bitcast.2, s32[32]{0:T(128)} %len_hbm.1, ...), custom_call_target="tpu_custom_call" | custom-call | tf_op jit(solution)/shard_map/attend_project/pallas_call | solution.py:586
  75.2 1.6 %copy.10 = bf16[16,5120]{1,0:T(8,128)(2,1)} copy(bf16[16,5120]{1,0:T(8,128)(2,1)} %attend_project.1) | data formatting | bytes 327680
